TPU v7x, 512 devices: a whole 4x8x8 slice. The times are simulated.
512 devices in a mesh: row: 16 (over x_lo, y), col: 32 (over x_hi, z, core).
Axes of the slice: x: 4 (x_hi: 2, x_lo: 2; x = x_hi * 2 + x_lo), y: 8, z: 8, core: 2. Of those that a mesh axis runs over, the one named last changes fastest.
Arguments:
- matrix: float32 [4096, 8192], P('row', 'col'), may hold values from -64 to 64
- right_factor: float32 [8192, 8192], P('row', 'col'), may hold values from -6 to 6
Outputs:
- rotated_matrix: float32 [4096, 8192], P('row', 'col')
- rotated_factor: float32 [8192, 8192], P('row', 'col')
All inputs are finite; a program needn't handle non-finite values.
Results may differ from a plain program's by a relative error of at most 0.0003.
Values sent between devices are 32-bit elements; how exact they have to be, the bound alone decides.
A program may use at most 64 MiB of HBM per device.

v0:
```python
import jax
import jax.numpy as jnp
import numpy as np
from jax import lax
from jax.sharding import PartitionSpec as P

BLK = 128
ROUNDS = 6
STEPS = 2


def shifted(value, axis, steps):
    count = lax.axis_size(axis)
    first, last = (max(0, -steps), min(count, count - steps))
    return lax.ppermute(value, axis, [(source, source + steps) for source in range(first, last)])


def gram_of(block):
    return lax.dot_general(
        block,
        block,
        (((0,), (0,)), ((), ())),
        precision=lax.Precision.HIGHEST,
        preferred_element_type=jnp.float32,
    )


def times_rotation(block, rotation):
    return jnp.dot(
        block, rotation, precision=lax.Precision.HIGHEST, preferred_element_type=jnp.float32
    )


def permute(values, round_index, axis):
    order = values.shape[axis]
    last_index = order - 1
    head = lax.slice_in_dim(values, 0, last_index, axis=axis)
    moved = jnp.roll(jnp.flip(head, axis), (2 * round_index - order + 2) % last_index, axis)
    before = lax.slice_in_dim(moved, 0, round_index, axis=axis)
    after = lax.slice_in_dim(moved, round_index + 1, last_index, axis=axis)
    fixed = lax.slice_in_dim(values, last_index, order, axis=axis)
    tail = lax.slice_in_dim(values, round_index, round_index + 1, axis=axis)
    return jnp.concatenate([before, fixed, after, tail], axis=axis)


def rotation_round(round_index, gram_pair, rotation):
    order = gram_pair.shape[0]
    indices = np.arange(order)
    last_index = order - 1
    partner = np.where(
        indices == last_index,
        round_index,
        np.where(indices == round_index, last_index, np.mod(2 * round_index - indices, last_index)),
    )
    lower_side = jnp.asarray(indices < partner)
    diagonal = jnp.diagonal(gram_pair)
    columns = permute(gram_pair, round_index, 1)
    across = jnp.diagonal(columns)
    spread = permute(diagonal, round_index, 0) - diagonal
    sign_of = jnp.where(spread >= 0, 1.0, -1.0).astype(gram_pair.dtype)
    half_angle = 0.5 * sign_of * jnp.arctan2(2.0 * across, jnp.abs(spread))
    angle = jnp.where(lower_side, half_angle, permute(half_angle, round_index, 0))
    cosine = jnp.cos(angle)
    sine = jnp.sin(angle)
    signed = jnp.where(lower_side, -sine, sine)
    mixed = gram_pair * cosine[None, :] + columns * signed[None, :]
    gram_pair = mixed * cosine[:, None] + permute(mixed, round_index, 0) * signed[:, None]
    rotation = rotation * cosine[None, :] + permute(rotation, round_index, 1) * signed[None, :]
    return (gram_pair, rotation)


def inner_solve(gram_pair):
    rotation = jnp.eye(gram_pair.shape[0], dtype=gram_pair.dtype)
    for round_index in range(ROUNDS):
        gram_pair, rotation = rotation_round(round_index, gram_pair, rotation)
    return (gram_pair, rotation)


def advance(slab, factor):
    position = lax.axis_index("col")
    width_col = lax.axis_size("col")
    outgoing_slab = jnp.where(position == 0, slab[:, BLK:], slab[:, :BLK])
    outgoing_factor = jnp.where(position == 0, factor[:, BLK:], factor[:, :BLK])
    arrived = shifted((outgoing_slab, outgoing_factor), "col", 1)
    returned = shifted((slab[:, BLK:], factor[:, BLK:]), "col", -1)
    upper_slab = jnp.where(position == 0, slab[:, :BLK], arrived[0])
    upper_factor = jnp.where(position == 0, factor[:, :BLK], arrived[1])
    lower_slab = jnp.where(position == width_col - 1, slab[:, :BLK], returned[0])
    lower_factor = jnp.where(position == width_col - 1, factor[:, :BLK], returned[1])
    return (
        jnp.concatenate([upper_slab, lower_slab], axis=1),
        jnp.concatenate([upper_factor, lower_factor], axis=1),
    )


def shards(matrix, right_factor):
    slab = matrix
    factor = right_factor
    gram_pair = lax.psum(gram_of(slab), "row")
    for section in range(STEPS):
        rotated_gram, rotation = inner_solve(gram_pair)
        slab = times_rotation(slab, rotation)
        factor = times_rotation(factor, rotation)
        if section + 1 == STEPS:
            slab, factor = advance(slab, factor)
        else:
            slab, factor = advance(slab, factor)
            gram_pair = lax.psum(gram_of(slab), "row")
    return (slab, factor)


def solution(mesh):
    in_specs = (P("row", "col"), P("row", "col"))
    out_specs = (P("row", "col"), P("row", "col"))
    return jax.shard_map(shards, mesh=mesh, in_specs=in_specs, out_specs=out_specs, check_vma=False)
```

profile of v0, /device:TPU:4, one launch (start us, length us, event | category | flops | bytes accessed | tf_op | source)
XLA Modules:
  0.0 548.0 jit_solution(16968387984603803168)
XLA Ops:
  7.2 2.4 fusion.206
  10.5 144.5 %all-reduce.3.cloned.1.call-done = f32[256,256]{1,0:T(8,128)} async-done(((f32[256,256]{1,0:T(8,128)}), f32[256,256]{1,0:T(8,128)}) %all-reduce.3.cloned.1.call-update) | async-done | bytes 262160 | tf_op jit(solution)/shard_map/psum | solution.py:99
  155.0 2.6 gather_fusion
  159.2 2.3 gather_fusion.1
  161.7 1.4 fusion.111
  164.6 1.4 fusion.148
  167.0 2.3 gather_fusion.2
  172.8 2.3 gather_fusion.3
  175.8 2.1 fusion.113
  180.8 2.1 fusion.147
  186.4 2.3 gather_fusion.4
  192.1 2.3 gather_fusion.5
  195.2 1.4 fusion.115
  199.3 1.4 fusion.146
  204.5 2.3 gather_fusion.6
  210.2 2.3 gather_fusion.7
  213.4 1.4 fusion.117
  217.4 1.4 fusion.145
  222.7 2.3 gather_fusion.8
  228.8 2.3 gather_fusion.9
  232.0 1.4 fusion.119
  236.0 1.4 fusion.144
  241.3 2.3 gather_fusion.10
  247.0 2.3 gather_fusion.11
  250.1 1.4 fusion.121
  254.6 1.4 fusion.143
  258.5 1.1 convolution_bitcast_fusion
  259.6 1.9 collective-permute-start
  261.6 7.3 %collective-permute-start.1 = (f32[256,128]{0,1:T(8,128)S(1)}, f32[256,128]{0,1:T(8,128)S(1)}, u32[]{:S(2)}, u32[]{:S(2)}) collective-permute-start(f32[256,128]{0,1:T(8,128)S(1)} %get-tuple-element.80), channel_id=1, source_target_pairs={{1,0},{2,1},{3,2},{4,3},{5,4},{6,5},{7,6},{8,7},{9,8},{10,9},{11,1... | collective-permute-start | bytes 393224 | tf_op jit(solution)/shard_map/ppermute | solution.py:15
  268.9 1.9 collective-permute-start.4
  270.8 7.3 %collective-permute-start.5 = (f32[512,128]{0,1:T(8,128)S(1)}, f32[512,128]{0,1:T(8,128)S(1)}, u32[]{:S(2)}, u32[]{:S(2)}) collective-permute-start(f32[512,128]{0,1:T(8,128)S(1)} %get-tuple-element.37), channel_id=1, source_target_pairs={{1,0},{2,1},{3,2},{4,3},{5,4},{6,5},{7,6},{8,7},{9,8},{10,9},{11,1... | collective-permute-start | bytes 786440 | tf_op jit(solution)/shard_map/ppermute | solution.py:15
  278.1 1.1 fusion.109
  280.2 1.8 collective-permute-done.5
  282.0 129.6 %all-reduce.5.cloned.1.call-done = f32[256,256]{1,0:T(8,128)} async-done(((f32[256,256]{1,0:T(8,128)}), f32[256,256]{1,0:T(8,128)}) %all-reduce.5.cloned.1.call-update) | async-done | bytes 262160 | tf_op jit(solution)/shard_map/psum | solution.py:108
  411.6 2.6 gather_fusion.12
  416.0 2.3 gather_fusion.13
  418.5 1.4 fusion.123
  420.8 1.4 fusion.142
  423.1 2.3 gather_fusion.14
  428.6 2.3 gather_fusion.15
  431.7 2.1 fusion.125
  436.7 2.1 fusion.141
  444.4 2.3 gather_fusion.16
  450.1 2.3 gather_fusion.17
  453.2 1.4 fusion.127
  457.3 1.4 fusion.140
  462.6 2.3 gather_fusion.18
  468.3 2.3 gather_fusion.19
  471.4 1.4 fusion.129
  475.4 1.4 fusion.139
  480.7 2.3 gather_fusion.20
  486.4 2.3 gather_fusion.21
  489.5 1.4 fusion.131
  493.6 1.4 fusion.138
  500.3 2.3 gather_fusion.22
  506.0 2.3 gather_fusion.23
  509.1 1.4 fusion.133
  513.5 1.4 fusion.137
  516.8 1.9 collective-permute-start.2
  518.8 7.3 %collective-permute-start.3 = (f32[256,128]{0,1:T(8,128)S(1)}, f32[256,128]{0,1:T(8,128)S(1)}, u32[]{:S(2)}, u32[]{:S(2)}) collective-permute-start(f32[256,128]{0,1:T(8,128)S(1)} %get-tuple-element.41), channel_id=1, source_target_pairs={{1,0},{2,1},{3,2},{4,3},{5,4},{6,5},{7,6},{8,7},{9,8},{10,9},{11,1... | collective-permute-start | bytes 393224 | tf_op jit(solution)/shard_map/ppermute | solution.py:15
  526.8 1.9 collective-permute-start.6
  528.7 7.3 %collective-permute-start.7 = (f32[512,128]{0,1:T(8,128)S(1)}, f32[512,128]{0,1:T(8,128)S(1)}, u32[]{:S(2)}, u32[]{:S(2)}) collective-permute-start(f32[512,128]{0,1:T(8,128)S(1)} %get-tuple-element.33), channel_id=1, source_target_pairs={{1,0},{2,1},{3,2},{4,3},{5,4},{6,5},{7,6},{8,7},{9,8},{10,9},{11,1... | collective-permute-start | bytes 786440 | tf_op jit(solution)/shard_map/ppermute | solution.py:15
  536.9 1.2 collective-permute-done.6
  538.1 1.8 collective-permute-done.7
  (677 shorter events, 117.3 us)
Async XLA Ops:
  7.2 251.4 %copy-start = (f32[512,256]{1,0:T(8,128)S(1)}, f32[512,256]{1,0:T(8,128)}, u32[]{:S(2)}) copy-start(f32[512,256]{1,0:T(8,128)} %param.15) | copy-start | bytes 1572868
  7.2 147.8 %all-reduce.3.cloned.1.call-start = ((), (), s32[]{:S(2)}) async-start(), calls=%async_computation | async-start | bytes 524288 | tf_op jit(solution)/shard_map/psum | solution.py:99
  9.6 402.0 %all-reduce.5.cloned.1.call-start = ((), (), s32[]{:S(2)}) async-start(), calls=%async_computation.1 | async-start | bytes 524288 | tf_op jit(solution)/shard_map/psum | solution.py:108
  155.0 3.3 copy-start.1
  175.1 0.7 copy-start.26
  183.0 0.7 copy-start.13
  183.9 0.7 slice-start.5
  185.1 1.0 copy-start.14
  188.7 1.1 copy-start.49
  194.5 0.7 copy-start.50
  196.7 0.8 copy-start.33
  198.6 0.7 copy-start.67
  200.8 0.7 copy-start.7
  201.9 0.7 slice-start.2
  203.3 1.0 copy-start.8
  206.9 1.1 copy-start.51
  214.8 0.8 copy-start.35
  216.7 0.7 copy-start.65
  218.9 0.7 copy-start.15
  220.1 0.7 slice-start.6
  221.4 1.0 copy-start.16
  225.0 1.1 copy-start.53
  233.4 0.8 copy-start.37
  237.6 0.7 copy-start.3
  238.7 0.7 slice-start
  240.0 1.0 copy-start.4
  243.7 1.1 copy-start.47
  251.6 0.8 copy-start.29
  257.0 1.0 copy-start.19
  259.6 18.4 %collective-permute-start = (f32[256,128]{0,1:T(8,128)S(1)}, f32[256,128]{0,1:T(8,128)S(1)}, u32[]{:S(2)}, u32[]{:S(2)}) collective-permute-start(f32[256,128]{0,1:T(8,128)S(1)} %get-tuple-element.79), channel_id=1, source_target_pairs={{0,1},{1,2},{2,3},{3,4},{4,5},{5,6},{6,7},{7,8},{8,9},{9,10},{10,1... | collective-permute-start | bytes 393224 | tf_op jit(solution)/shard_map/ppermute | solution.py:15
  261.6 16.5 %collective-permute-start.1 = (f32[256,128]{0,1:T(8,128)S(1)}, f32[256,128]{0,1:T(8,128)S(1)}, u32[]{:S(2)}, u32[]{:S(2)}) collective-permute-start(f32[256,128]{0,1:T(8,128)S(1)} %get-tuple-element.80), channel_id=1, source_target_pairs={{1,0},{2,1},{3,2},{4,3},{5,4},{6,5},{7,6},{8,7},{9,8},{10,9},{11,1... | collective-permute-start | bytes 393224 | tf_op jit(solution)/shard_map/ppermute | solution.py:15
  268.9 11.3 %collective-permute-start.4 = (f32[512,128]{0,1:T(8,128)S(1)}, f32[512,128]{0,1:T(8,128)S(1)}, u32[]{:S(2)}, u32[]{:S(2)}) collective-permute-start(f32[512,128]{0,1:T(8,128)S(1)} %get-tuple-element.36), channel_id=1, source_target_pairs={{0,1},{1,2},{2,3},{3,4},{4,5},{5,6},{6,7},{7,8},{8,9},{9,10},{10,1... | collective-permute-start | bytes 786440 | tf_op jit(solution)/shard_map/ppermute | solution.py:15
  270.8 11.1 %collective-permute-start.5 = (f32[512,128]{0,1:T(8,128)S(1)}, f32[512,128]{0,1:T(8,128)S(1)}, u32[]{:S(2)}, u32[]{:S(2)}) collective-permute-start(f32[512,128]{0,1:T(8,128)S(1)} %get-tuple-element.37), channel_id=1, source_target_pairs={{1,0},{2,1},{3,2},{4,3},{5,4},{6,5},{7,6},{8,7},{9,8},{10,9},{11,1... | collective-permute-start | bytes 786440 | tf_op jit(solution)/shard_map/ppermute | solution.py:15
  411.6 3.3 copy-start.2
  431.0 0.7 copy-start.28
  438.8 0.7 copy-start.11
  441.1 0.7 slice-start.4
  442.2 0.9 copy-start.20
  443.1 0.9 copy-start.12
  443.1 1.0 copy-start.72
  443.1 1.0 copy-start.73
  443.3 0.8 copy-start.71
  446.8 1.1 copy-start.55
  454.7 0.8 copy-start.39
  456.6 0.7 copy-start.68
  458.8 0.7 copy-start.9
  459.9 0.7 slice-start.3
  461.3 1.0 copy-start.10
  464.9 1.1 copy-start.57
  472.8 0.8 copy-start.41
  477.0 0.7 copy-start.17
  478.1 0.7 slice-start.7
  479.4 1.0 copy-start.18
  483.1 1.1 copy-start.59
  491.0 0.8 copy-start.43
  495.1 0.7 copy-start.5
  496.2 0.8 slice-start.1
  498.3 1.0 copy-start.6
  502.6 1.1 copy-start.45
  510.5 0.8 copy-start.31
  516.8 19.1 %collective-permute-start.2 = (f32[256,128]{0,1:T(8,128)S(1)}, f32[256,128]{0,1:T(8,128)S(1)}, u32[]{:S(2)}, u32[]{:S(2)}) collective-permute-start(f32[256,128]{0,1:T(8,128)S(1)} %get-tuple-element.40), channel_id=1, source_target_pairs={{0,1},{1,2},{2,3},{3,4},{4,5},{5,6},{6,7},{7,8},{8,9},{9,10},{10,1... | collective-permute-start | bytes 393224 | tf_op jit(solution)/shard_map/ppermute | solution.py:15
  518.8 17.2 %collective-permute-start.3 = (f32[256,128]{0,1:T(8,128)S(1)}, f32[256,128]{0,1:T(8,128)S(1)}, u32[]{:S(2)}, u32[]{:S(2)}) collective-permute-start(f32[256,128]{0,1:T(8,128)S(1)} %get-tuple-element.41), channel_id=1, source_target_pairs={{1,0},{2,1},{3,2},{4,3},{5,4},{6,5},{7,6},{8,7},{9,8},{10,9},{11,1... | collective-permute-start | bytes 393224 | tf_op jit(solution)/shard_map/ppermute | solution.py:15
  526.8 11.3 %collective-permute-start.6 = (f32[512,128]{0,1:T(8,128)S(1)}, f32[512,128]{0,1:T(8,128)S(1)}, u32[]{:S(2)}, u32[]{:S(2)}) collective-permute-start(f32[512,128]{0,1:T(8,128)S(1)} %get-tuple-element.32), channel_id=1, source_target_pairs={{0,1},{1,2},{2,3},{3,4},{4,5},{5,6},{6,7},{7,8},{8,9},{9,10},{10,1... | collective-permute-start | bytes 786440 | tf_op jit(solution)/shard_map/ppermute | solution.py:15
  528.7 11.1 %collective-permute-start.7 = (f32[512,128]{0,1:T(8,128)S(1)}, f32[512,128]{0,1:T(8,128)S(1)}, u32[]{:S(2)}, u32[]{:S(2)}) collective-permute-start(f32[512,128]{0,1:T(8,128)S(1)} %get-tuple-element.33), channel_id=1, source_target_pairs={{1,0},{2,1},{3,2},{4,3},{5,4},{6,5},{7,6},{8,7},{9,8},{10,9},{11,1... | collective-permute-start | bytes 786440 | tf_op jit(solution)/shard_map/ppermute | solution.py:15
  (48 other events, 31.7 us)
Sparse Core Ops, SparseCore 0:
  11.5 143.4 all-reduce.2
  279.4 132.1 all-reduce.4
where the time goes:
time: 559 us; the launch traced here: 548 us
  waiting for transfers between devices  280 us (50%)
  local copies, waits for them, and re-layouts  161 us (29%)
  other arithmetic  47.2 us (8%)
  starting transfers between devices  36.8 us (7%)
  between operations  16.7 us (3%)
  matrix products  6.43 us (1%)
    psum x2, waiting for transfers between devices, shards(): gram_pair = lax.psum(gram_of(slab), 'row')  274 us
    unnamed x244, local copies, waits for them, and re-layouts  45 us
    ppermute x8, starting transfers between devices, shifted(): lax.ppermute(value, axis, [(source, source + steps) for source in range(f...  36.7 us
    slice x191, local copies, waits for them, and re-layouts, permute(): jnp.roll(jnp.flip(head, axis), (2 * round_index - order + 2) % last_index...  30.8 us
    gather x12, local copies, waits for them, and re-layouts, rotation_round(): diagonal = jnp.diagonal(gram_pair)  28.7 us
    gather x12, local copies, waits for them, and re-layouts, rotation_round(): across = jnp.diagonal(columns)  28.1 us
    cos x12, other arithmetic, rotation_round(): cosine = jnp.cos(angle)  18.6 us
    mul x12, other arithmetic, rotation_round(): half_angle = 0.5 * sign_of * jnp.arctan2(2.0 * across, jnp.abs(spread))  18.5 us
  transfers between devices with their start and end apart: 10, of which 6 were waited for; matrix products, arithmetic and copies ran while one was open for 1% of the time, Pallas kernels for 0%

commit v1 on v0

v1 whole, which is shorter than its diff:
```python
import jax
import jax.numpy as jnp
from jax import lax
from jax.experimental import pallas as pl
from jax.experimental.pallas import tpu as pltpu
from jax.sharding import PartitionSpec as P

BLK = 128
ROUNDS = 6
ROWS = 8
KEPT = 6
MESH = pl.DeviceIdType.MESH
F32 = jnp.float32


def iota(shape, axis):
    return lax.broadcasted_iota(jnp.int32, shape, axis)


def next_lane(x):
    return pltpu.roll(x, BLK - 1, 1)


def previous_lane(x):
    return pltpu.roll(x, 1, 1)


def below(x, n):
    even, odd = x
    up_even, up_odd = pltpu.roll(even, ROWS - 1, 0), pltpu.roll(odd, ROWS - 1, 0)
    return (odd, up_even) if n == 1 else (up_even, up_odd)


def above(x, n):
    even, odd = x
    down_even, down_odd = pltpu.roll(even, 1, 0), pltpu.roll(odd, 1, 0)
    return (down_odd, even) if n == 1 else (down_even, down_odd)


def both(function, *operands):
    return tuple(function(*parts) for parts in zip(*operands))


def lanes(x, index):
    return jnp.take_along_axis(x, jnp.broadcast_to(index, x.shape), axis=1)


def halves(x):
    high = x.astype(jnp.bfloat16)
    return high, (x - high.astype(F32)).astype(jnp.bfloat16)


def dot(x, y):
    return jnp.dot(x, y, preferred_element_type=F32)


def times(x, split):
    x_high, x_low = halves(x)
    high, low = split
    return dot(x_high, high) + (dot(x_low, high) + dot(x_high, low))


def backwards(x):
    return lanes(x, BLK - 1 - iota((1, BLK), 1))


def diagonals(x, place):
    place[...] = pltpu.roll(x, 1, 1, stride=1, stride_axis=0).T[:2 * ROWS]
    return place[pl.ds(0, ROWS, stride=2)], place[pl.ds(1, ROWS, stride=2)]


def flipped_rows(x):
    index = jnp.clip(KEPT - 1 - iota(x.shape, 0), 0, ROWS - 1)
    return jnp.take_along_axis(x, index, axis=0)


def pack(even, odd):
    j, lane = iota((ROWS, BLK), 0), iota((ROWS, BLK), 1)
    odd = flipped_rows(odd)
    high = pltpu.roll(odd, 0, 1, stride=1, stride_axis=0)
    low = pltpu.roll(pltpu.roll(odd, 0, 1, stride=3, stride_axis=0), BLK - 11, 1)
    return jnp.where(lane < j, high, jnp.where(lane < 2 * j, low, even))[:KEPT]


def unpack(packed):
    i, lane = iota((ROWS, BLK), 0), iota((ROWS, BLK), 1)
    back = flipped_rows(packed)
    high = pltpu.roll(pltpu.roll(back, 0, 1, stride=1, stride_axis=0), BLK - 5, 1)
    low = pltpu.roll(pltpu.roll(back, 0, 1, stride=3, stride_axis=0), BLK - 4, 1)
    return packed, jnp.where(lane >= BLK - 5 + i, high, low)


def gram_bands(upper, lower, place):
    left = jnp.concatenate([upper, backwards(lower)], axis=1)
    right = jnp.concatenate([backwards(upper), lower], axis=1)
    gram = lax.dot_general(
        left, right, (((0,), (0,)), ((), ())), precision=lax.Precision.HIGHEST, preferred_element_type=F32
    )
    blocks = (gram[:BLK, :BLK], gram[:BLK, BLK:], gram[BLK:, :BLK], gram[BLK:, BLK:])
    return [pack(*diagonals(block, place.at[at])) for at, block in enumerate(blocks)]


def angles(round_index, uu, uv, vv):
    lane = iota((1, BLK), 1)
    spread = vv[0][0:1] - uu[0][0:1]
    across = 2.0 * uv[0][0:1]
    width = jnp.abs(spread)
    scale = jnp.maximum(jnp.abs(across), width)
    live = scale > 0
    inverse = 1.0 / jnp.where(live, scale, 1.0)
    across = across * inverse
    width = jnp.where(live, width * inverse, 1.0)
    root = lax.rsqrt(across * across + width * width)
    square = 0.5 + 0.5 * width * root
    root_cosine = lax.rsqrt(square)
    cosine = square * root_cosine
    sine = 0.5 * across * root * root_cosine
    upper_first = (lane == 0) | (lane > round_index)
    positive = (spread > 0) | ((spread == 0) & upper_first)
    return cosine, jnp.where(positive, sine, -sine)


def shift_pairs(uu, uv, vu, vv):
    lane, row = iota((ROWS, BLK), 1), iota((ROWS, BLK), 0)
    last, first, second = lane == BLK - 1, lane == 0, lane == 1
    uu_next, uv_next = both(next_lane, uu), both(next_lane, uv)
    uu_back, uv_back, vu_back, vv_back = (both(previous_lane, x) for x in (uu, uv, vu, vv))
    vu_1, vv_b1, uv_n1 = above(vu, 1), below(vv, 1), below(uv_next, 1)
    uu_n2, uv_n2, vu_b2, vv_b1up = below(uu_next, 2), below(uv_next, 2), above(vu_back, 2), above(vv_back, 1)
    uv_b1up = above(uv_back, 1)
    out = []
    for at in range(2):
        q = 2 * row + at
        new_uu = jnp.where(last, vu_1[at] if at else jnp.where(q == 0, vv[at], vu_1[at]), uu_next[at])
        new_uv = jnp.where(q == lane - 1, uu_n2[at], uv_n2[at])
        new_uv = jnp.where(q == lane, uv_n1[at], new_uv)
        new_uv = jnp.where(last, vv_b1[at], new_uv)
        if at:
            new_vu = jnp.where(q == 1, jnp.where(second, uu[at], uv[at]), vu_b2[at])
        else:
            new_vu = jnp.where(q == 0, new_uv, vu_b2[at])
        new_vv = jnp.where(q == lane - 1, vu_back[at], vv_back[at])
        new_vv = jnp.where(q == lane, vv_b1up[at], new_vv)
        new_vv = jnp.where(first, vv[at], new_vv)
        new_vv = jnp.where(second & (q == at), uv_b1up[at] if at else uu_back[at], new_vv)
        out.append((new_uu, new_uv, new_vu, new_vv))
    return tuple(zip(*out))


def solve(uu, uv, vu, vv):
    tall = (2 * BLK, BLK)
    row, lane = iota(tall, 0), iota(tall, 1)
    q_u = jnp.where(row == lane, 1.0, 0.0).astype(F32)
    q_v = jnp.where(row == 2 * BLK - 1 - lane, 1.0, 0.0).astype(F32)
    for round_index in range(ROUNDS):
        cos, sin = angles(round_index, uu, uv, vv)
        q_u, q_v = q_u * cos - q_v * sin, q_u * sin + q_v * cos
        if round_index + 1 == ROUNDS:
            break
        near = [jnp.broadcast_to(x, (ROWS, BLK)) for x in (cos, sin)]
        new = []
        for at in range(2):
            far_cos, far_sin = (pltpu.roll(x, at, 1, stride=2, stride_axis=0) for x in near)
            a, b, c, d = uu[at], uv[at], vu[at], vv[at]
            a, b = a * far_cos - b * far_sin, a * far_sin + b * far_cos
            c, d = c * far_cos - d * far_sin, c * far_sin + d * far_cos
            a, c = a * cos - c * sin, a * sin + c * cos
            b, d = b * cos - d * sin, b * sin + d * cos
            new.append((a, b, c, d))
        uu, uv, vu, vv = shift_pairs(*zip(*new))
        q_u, q_v = (
            jnp.where(lane == BLK - 1, q_v, next_lane(q_u)),
            jnp.where(lane == 0, q_v, jnp.where(lane == 1, previous_lane(q_u), previous_lane(q_v))),
        )
    return q_u, q_v


def block_columns(q_u, q_v, lower):
    last_round = ROUNDS - 1
    lane = iota((1, BLK), 1)
    upper_index = jnp.where(lane >= last_round, lane - last_round, last_round - lane)
    from_u = jnp.where(lane < last_round, BLK - last_round + lane, 0)
    from_v = jnp.where(lane == BLK - 1, 0, BLK - 1 + last_round - lane)
    lower_index = jnp.where(lane < last_round, from_u, from_v)
    index = jnp.where(lower, lower_index, upper_index)
    first = lane < last_round
    in_u = (first & lower) | (jnp.logical_not(first) & jnp.logical_not(lower))
    return jnp.where(in_u, lanes(q_u, index), lanes(q_v, index))


def kernel(
    rows, pairs,
    s_in, f_in, s_out, f_out,
    s_own, f_own, s_half, f_half, s_pair, f_pair, s_done, f_done, bands, place, total,
    load_sem, store_sem, sum_send, sum_recv, move_send, move_recv,
):
    row, col = lax.axis_index("row"), lax.axis_index("col")
    last = pairs - 1

    load_s = pltpu.make_async_copy(s_in, s_own, load_sem.at[0])
    load_f = pltpu.make_async_copy(f_in, f_own, load_sem.at[1])
    load_s.start()
    load_f.start()

    up_to = jnp.where(col == 0, 1, jnp.where(col == last, last - 1, jnp.where(col == last - 1, last, col + 2)))
    up_pair = jnp.where(col >= last - 1, 1, 0)
    up_half = jnp.where(col == last, 1, 0)
    low_to = jnp.where(col == 0, 2, jnp.where(col == 1, 0, col - 2))
    low_pair = jnp.where(col <= 1, 0, 1)
    low_half = jnp.where(col == 0, 0, 1)
    stays_a = jnp.where(col == 0, 0, 1)
    stays_b = jnp.where(col == 0, 1, 0)
    half_b = jnp.where(col == last, 1, 0)

    barrier = pltpu.get_barrier_semaphore()
    peers = [lax.rem(row + rows // 2 * (d % 2) + d // 2, rows) for d in range(rows - 1, 0, -1)]
    for peer in peers:
        pl.semaphore_signal(barrier, inc=1, device_id={"row": peer}, device_id_type=MESH)
    for partner in (up_to, low_to):
        pl.semaphore_signal(barrier, inc=1, device_id={"col": partner}, device_id_type=MESH)

    def send(at, source, target, peer):
        return pltpu.make_async_remote_copy(
            src_ref=source, dst_ref=target, send_sem=sum_send.at[at], recv_sem=sum_recv.at[at],
            device_id={"row": peer}, device_id_type=MESH,
        )

    def share(at):
        own = bands.at[at, row]
        for peer in peers:
            send(at, own, own, peer).start()

    def form(at, upper, lower):
        for block, packed in enumerate(gram_bands(upper, lower, place)):
            bands[at, row, KEPT * block:KEPT * (block + 1)] = packed

    def summed(at):
        rest = bands.at[at, pl.ds(0, rows - 1)]
        with jax.named_scope("sum_wait"):
            send(at, rest, rest, peers[0]).wait_recv()
        whole = bands[at, 0]
        for d in range(1, rows):
            whole = whole + bands[at, d]
        total[at, 0:4 * KEPT] = whole
        return [unpack(total[at, KEPT * block:KEPT * block + ROWS]) for block in range(4)]

    total[...] = jnp.zeros(total.shape, F32)
    with jax.named_scope("load_slab"):
        load_s.wait()
    with jax.named_scope("gram_first"):
        form(0, s_own[:, :BLK], s_own[:, BLK:])
    with jax.named_scope("entry"):
        pl.semaphore_wait(barrier, rows + 1)
    share(0)
    blocks = summed(0)
    with jax.named_scope("solve_first"):
        q_u, q_v = solve(*blocks)
        split = [halves(block_columns(q_u, q_v, lower)) for lower in (False, True)]
        split = [jnp.concatenate(parts, axis=1) for parts in zip(*split)]

    def move(kind, half, at, target, pair, half_at, to):
        return pltpu.make_async_remote_copy(
            src_ref=half.at[at], dst_ref=target.at[pair, half_at],
            send_sem=move_send.at[kind, at], recv_sem=move_recv.at[kind, pair],
            device_id={"col": to}, device_id_type=MESH,
        )

    def moves(kind, half, target):
        return (
            move(kind, half, 0, target, up_pair, up_half, up_to),
            move(kind, half, 1, target, low_pair, low_half, low_to),
        )

    def rotate(own, half, target):
        moved = times(own[...], split)
        half[0] = moved[:, :BLK]
        half[1] = moved[:, BLK:]

    def stay(half, target):
        target[0, stays_a] = half[stays_a]
        target[1, half_b] = half[stays_b]

    s_moves, f_moves = moves(0, s_half, s_pair), moves(1, f_half, f_pair)
    with jax.named_scope("apply_slab"):
        rotate(s_own, s_half, s_pair)
    for copy in s_moves:
        copy.start()
    load_f.wait()
    with jax.named_scope("apply_factor"):
        stay(s_half, s_pair)
        rotate(f_own, f_half, f_pair)
        stay(f_half, f_pair)

    def arrived(kind, half, target, pair):
        move(kind, half, 0, target, pair, 0, up_to).wait_recv()

    for pair in range(2):
        with jax.named_scope("slab_arrival"):
            arrived(0, s_half, s_pair, pair)
        with jax.named_scope("gram_second"):
            form(1 + pair, s_pair[pair, 0], s_pair[pair, 1])
        share(1 + pair)
    for copy in f_moves:
        copy.start()

    lower_of = (col == 1, col != last)

    def finish(target, done, pair, split):
        whole = jnp.concatenate([target[pair, 0], target[pair, 1]], axis=1)
        done[:, pair * BLK:(pair + 1) * BLK] = times(whole, split)

    splits = []
    for pair in range(2):
        blocks = summed(1 + pair)
        with jax.named_scope("solve_second"):
            q_u, q_v = solve(*blocks)
            splits.append(halves(block_columns(q_u, q_v, lower_of[pair])))
        with jax.named_scope("finish_slab"):
            finish(s_pair, s_done, pair, splits[pair])
    store_s = pltpu.make_async_copy(s_done, s_out, store_sem.at[0])
    store_s.start()
    for pair in range(2):
        with jax.named_scope("factor_arrival"):
            arrived(1, f_half, f_pair, pair)
        with jax.named_scope("finish_factor"):
            finish(f_pair, f_done, pair, splits[pair])
    store_f = pltpu.make_async_copy(f_done, f_out, store_sem.at[1])
    store_f.start()

    with jax.named_scope("last_waits"):
        for copy in s_moves + f_moves:
            copy.wait_send()
        for at in range(3):
            rest = bands.at[at, pl.ds(0, rows - 1)]
            send(at, rest, rest, peers[0]).wait_send()
        store_s.wait()
        store_f.wait()


def solution(mesh):
    rows, pairs = mesh.shape["row"], mesh.shape["col"]

    def shards(matrix, right_factor):
        s_rows, f_rows = matrix.shape[0], right_factor.shape[0]
        return pl.pallas_call(
            lambda *refs: kernel(rows, pairs, *refs),
            out_shape=(
                jax.ShapeDtypeStruct(matrix.shape, F32),
                jax.ShapeDtypeStruct(right_factor.shape, F32),
            ),
            in_specs=[pl.BlockSpec(memory_space=pl.ANY)] * 2,
            out_specs=[pl.BlockSpec(memory_space=pl.ANY)] * 2,
            scratch_shapes=[
                pltpu.VMEM(matrix.shape, F32),
                pltpu.VMEM(right_factor.shape, F32),
                pltpu.VMEM((2, s_rows, BLK), F32),
                pltpu.VMEM((2, f_rows, BLK), F32),
                pltpu.VMEM((2, 2, s_rows, BLK), F32),
                pltpu.VMEM((2, 2, f_rows, BLK), F32),
                pltpu.VMEM(matrix.shape, F32),
                pltpu.VMEM(right_factor.shape, F32),
                pltpu.VMEM((3, rows, 4 * KEPT, BLK), F32),
                pltpu.VMEM((4, 2 * ROWS, BLK), F32),
                pltpu.VMEM((3, 4 * ROWS, BLK), F32),
                pltpu.SemaphoreType.DMA((2,)),
                pltpu.SemaphoreType.DMA((2,)),
                pltpu.SemaphoreType.DMA((3,)),
                pltpu.SemaphoreType.DMA((3,)),
                pltpu.SemaphoreType.DMA((2, 2)),
                pltpu.SemaphoreType.DMA((2, 2)),
            ],
            compiler_params=pltpu.CompilerParams(collective_id=0, has_side_effects=True),
            name="tournament",
        )(matrix, right_factor)

    spec = P("row", "col")
    return jax.shard_map(shards, mesh=mesh, in_specs=(spec, spec), out_specs=(spec, spec), check_vma=False)
```

time: 559 us -> 47.4 us (0.08)
  the two profiles are of different devices: /device:TPU:4 before, /device:TPU:12 now
where the time goes in v1:
time: 47.4 us; the launch traced here: 47.2 us
  Pallas kernels  44.1 us (93%)
  local copies, waits for them, and re-layouts  2.52 us (5%)
  between operations  0.65 us (1%)
    pallas_call x1, Pallas kernels, shards(): pl.pallas_call(lambda *refs: kernel(rows, pairs, *refs), out_shape=(jax.S...  44.1 us
    unnamed x4, local copies, waits for them, and re-layouts  2.52 us

profile of v1, /device:TPU:12, one launch (start us, length us, event | category | flops | bytes accessed | tf_op | source)
XLA Modules:
  0.0 47.2 jit_solution(1082352854416230521)
XLA Ops:
  0.6 44.1 %tournament.1 = (f32[256,256]{1,0:T(8,128)}, f32[512,256]{1,0:T(8,128)}) custom-call(f32[256,256]{1,0:T(8,128)} %refs_0_.1, f32[512,256]{1,0:T(8,128)} %refs_1_.1), custom_call_target="tpu_custom_call" | custom-call | tf_op jit(solution)/shard_map/tournament/pallas_call | solution.py:345
  44.7 0.0 copy-start
  44.7 1.7 %copy.6 = f32[256,256]{1,0:T(8,128)} copy(f32[256,256]{1,0:T(8,128)} %get-tuple-element.4) | data formatting | bytes 524288
  46.4 0.0 copy-done
  46.4 0.8 %copy.7 = f32[512,256]{1,0:T(8,128)} copy(f32[512,256]{1,0:T(8,128)S(1)} %copy-done) | data formatting | bytes 1048576
Async XLA Ops:
  44.7 1.7 %copy-start = (f32[512,256]{1,0:T(8,128)S(1)}, f32[512,256]{1,0:T(8,128)}, u32[]{:S(2)}) copy-start(f32[512,256]{1,0:T(8,128)} %get-tuple-element.5) | copy-start | bytes 1572868

commit v2 on v1

--- a/solution.py
+++ b/solution.py
@@ -9,6 +9,7 @@
 ROUNDS = 6
 ROWS = 8
 KEPT = 6
+GRANT = 32 * 1024 * 1024
 MESH = pl.DeviceIdType.MESH
 F32 = jnp.float32
 
@@ -54,10 +55,21 @@
     return jnp.dot(x, y, preferred_element_type=F32)
 
 
-def times(x, split):
-    x_high, x_low = halves(x)
+def times(x_split, split):
+    x_high, x_low = x_split
     high, low = split
     return dot(x_high, high) + (dot(x_low, high) + dot(x_high, low))
+
+
+def products(x, y):
+    x_high, x_low = halves(x)
+    y_high, y_low = halves(y)
+
+    def columns(a, b):
+        return lax.dot_general(a, b, (((0,), (0,)), ((), ())), preferred_element_type=F32)
+
+    small = columns(x_high, y_low) + columns(x_low, y_high)
+    return columns(x_high, y_high) + (small + columns(x_low, y_low))
 
 
 def backwards(x):
@@ -93,9 +105,7 @@
 def gram_bands(upper, lower, place):
     left = jnp.concatenate([upper, backwards(lower)], axis=1)
     right = jnp.concatenate([backwards(upper), lower], axis=1)
-    gram = lax.dot_general(
-        left, right, (((0,), (0,)), ((), ())), precision=lax.Precision.HIGHEST, preferred_element_type=F32
-    )
+    gram = products(left, right)
     blocks = (gram[:BLK, :BLK], gram[:BLK, BLK:], gram[BLK:, :BLK], gram[BLK:, BLK:])
     return [pack(*diagonals(block, place.at[at])) for at, block in enumerate(blocks)]
 
@@ -191,7 +201,7 @@
 def kernel(
     rows, pairs,
     s_in, f_in, s_out, f_out,
-    s_own, f_own, s_half, f_half, s_pair, f_pair, s_done, f_done, bands, place, total,
+    s_own, f_own, s_half, f_half, s_pair, f_pair, s_split, f_split, s_done, f_done, bands, place, total,
     load_sem, store_sem, sum_send, sum_recv, move_send, move_recv,
 ):
     row, col = lax.axis_index("row"), lax.axis_index("col")
@@ -214,10 +224,11 @@
 
     barrier = pltpu.get_barrier_semaphore()
     peers = [lax.rem(row + rows // 2 * (d % 2) + d // 2, rows) for d in range(rows - 1, 0, -1)]
-    for peer in peers:
-        pl.semaphore_signal(barrier, inc=1, device_id={"row": peer}, device_id_type=MESH)
-    for partner in (up_to, low_to):
-        pl.semaphore_signal(barrier, inc=1, device_id={"col": partner}, device_id_type=MESH)
+    with jax.named_scope("greet"):
+        for peer in peers:
+            pl.semaphore_signal(barrier, inc=1, device_id={"row": peer}, device_id_type=MESH)
+        for partner in (up_to, low_to):
+            pl.semaphore_signal(barrier, inc=1, device_id={"col": partner}, device_id_type=MESH)
 
     def send(at, source, target, peer):
         return pltpu.make_async_remote_copy(
@@ -272,7 +283,7 @@
         )
 
     def rotate(own, half, target):
-        moved = times(own[...], split)
+        moved = times(halves(own[...]), split)
         half[0] = moved[:, :BLK]
         half[1] = moved[:, BLK:]
 
@@ -305,26 +316,34 @@
 
     lower_of = (col == 1, col != last)
 
-    def finish(target, done, pair, split):
+    def keep_halves(target, pair, split):
         whole = jnp.concatenate([target[pair, 0], target[pair, 1]], axis=1)
-        done[:, pair * BLK:(pair + 1) * BLK] = times(whole, split)
-
-    splits = []
+        split[0, pair], split[1, pair] = halves(whole)
+
+    def finish(split, done, pair, rotation):
+        done[:, pair * BLK:(pair + 1) * BLK] = times((split[0, pair], split[1, pair]), rotation)
+
+    with jax.named_scope("split_slab"):
+        for pair in range(2):
+            keep_halves(s_pair, pair, s_split)
     for pair in range(2):
         blocks = summed(1 + pair)
         with jax.named_scope("solve_second"):
             q_u, q_v = solve(*blocks)
-            splits.append(halves(block_columns(q_u, q_v, lower_of[pair])))
+            rotation = halves(block_columns(q_u, q_v, lower_of[pair]))
         with jax.named_scope("finish_slab"):
-            finish(s_pair, s_done, pair, splits[pair])
+            finish(s_split, s_done, pair, rotation)
+        if pair == 0:
+            for at in range(2):
+                with jax.named_scope("factor_arrival"):
+                    arrived(1, f_half, f_pair, at)
+                with jax.named_scope("split_factor"):
+                    keep_halves(f_pair, at, f_split)
+        with jax.named_scope("finish_factor"):
+            finish(f_split, f_done, pair, rotation)
     store_s = pltpu.make_async_copy(s_done, s_out, store_sem.at[0])
+    store_f = pltpu.make_async_copy(f_done, f_out, store_sem.at[1])
     store_s.start()
-    for pair in range(2):
-        with jax.named_scope("factor_arrival"):
-            arrived(1, f_half, f_pair, pair)
-        with jax.named_scope("finish_factor"):
-            finish(f_pair, f_done, pair, splits[pair])
-    store_f = pltpu.make_async_copy(f_done, f_out, store_sem.at[1])
     store_f.start()
 
     with jax.named_scope("last_waits"):
@@ -337,16 +356,27 @@
         store_f.wait()
 
 
+def store(s_done, f_done, s_out, f_out, sem):
+    copies = [
+        pltpu.make_async_copy(source, target, sem.at[at])
+        for at, (source, target) in enumerate(((s_done, s_out), (f_done, f_out)))
+    ]
+    for copy in copies:
+        copy.start()
+    for copy in copies:
+        copy.wait()
+
+
 def solution(mesh):
     rows, pairs = mesh.shape["row"], mesh.shape["col"]
 
     def shards(matrix, right_factor):
         s_rows, f_rows = matrix.shape[0], right_factor.shape[0]
-        return pl.pallas_call(
+        done = pl.pallas_call(
             lambda *refs: kernel(rows, pairs, *refs),
             out_shape=(
-                jax.ShapeDtypeStruct(matrix.shape, F32),
-                jax.ShapeDtypeStruct(right_factor.shape, F32),
+                pltpu.VMEM(matrix.shape, F32),
+                pltpu.VMEM(right_factor.shape, F32),
             ),
             in_specs=[pl.BlockSpec(memory_space=pl.ANY)] * 2,
             out_specs=[pl.BlockSpec(memory_space=pl.ANY)] * 2,
@@ -357,6 +387,8 @@
                 pltpu.VMEM((2, f_rows, BLK), F32),
                 pltpu.VMEM((2, 2, s_rows, BLK), F32),
                 pltpu.VMEM((2, 2, f_rows, BLK), F32),
+                pltpu.VMEM((2, 2, s_rows, 2 * BLK), jnp.bfloat16),
+                pltpu.VMEM((2, 2, f_rows, 2 * BLK), jnp.bfloat16),
                 pltpu.VMEM(matrix.shape, F32),
                 pltpu.VMEM(right_factor.shape, F32),
                 pltpu.VMEM((3, rows, 4 * KEPT, BLK), F32),
@@ -369,9 +401,18 @@
                 pltpu.SemaphoreType.DMA((2, 2)),
                 pltpu.SemaphoreType.DMA((2, 2)),
             ],
-            compiler_params=pltpu.CompilerParams(collective_id=0, has_side_effects=True),
+            compiler_params=pltpu.CompilerParams(collective_id=0, has_side_effects=True, vmem_limit_bytes=GRANT),
             name="tournament",
-        )(matrix, right_factor)
+        )(*[pltpu.with_memory_space_constraint(x, pltpu.HBM) for x in (matrix, right_factor)])
+        return pl.pallas_call(
+            store,
+            out_shape=(pltpu.HBM(matrix.shape, F32), pltpu.HBM(right_factor.shape, F32)),
+            in_specs=[pl.BlockSpec(memory_space=pl.ANY)] * 2,
+            out_specs=[pl.BlockSpec(memory_space=pl.ANY)] * 2,
+            scratch_shapes=[pltpu.SemaphoreType.DMA((2,))],
+            compiler_params=pltpu.CompilerParams(vmem_limit_bytes=GRANT),
+            name="store",
+        )(*[pltpu.with_memory_space_constraint(x, pltpu.VMEM) for x in done])
 
     spec = P("row", "col")
     return jax.shard_map(shards, mesh=mesh, in_specs=(spec, spec), out_specs=(spec, spec), check_vma=False)

time: 47.4 us -> 44.3 us (0.935)
  local copies, waits for them, and re-layouts: 2.52 us -> 0 us
  Pallas kernels: 44.1 us -> 43.6 us
    unnamed x4 -> x0, local copies, waits for them, and re-layouts: 2.52 us -> none
    pallas_call x1 -> x2, Pallas kernels: 44.1 us -> 43.6 us  [the longest x1 42.7 us: shards(): pl.pallas_call(lambda *refs: kernel(rows, pairs, *refs), out_shape=(pltpu...]
where the time goes in v2:
time: 44.3 us; the launch traced here: 44.2 us
  Pallas kernels  43.6 us (98%)
  between operations  0.64 us (1%)
    pallas_call x1, Pallas kernels, shards(): pl.pallas_call(lambda *refs: kernel(rows, pairs, *refs), out_shape=(pltpu...  42.7 us
    pallas_call x1, Pallas kernels, shards(): pl.pallas_call(store, out_shape=(pltpu.HBM(matrix.shape, F32), pltpu.HBM(...  0.9 us

profile of v2, /device:TPU:12, one launch (start us, length us, event | category | flops | bytes accessed | tf_op | source)
XLA Modules:
  0.0 44.2 jit_solution(15648268049775716743)
XLA Ops:
  0.6 42.7 %tournament.1 = (f32[256,256]{1,0:T(8,128)S(1)}, f32[512,256]{1,0:T(8,128)S(1)}) custom-call(f32[256,256]{1,0:T(8,128)} %refs_0_.1, f32[512,256]{1,0:T(8,128)} %refs_1_.1), custom_call_target="tpu_custom_call" | custom-call | tf_op jit(solution)/shard_map/tournament/pallas_call | solution.py:375
  43.3 0.9 %store.1 = (f32[256,256]{1,0:T(8,128)}, f32[512,256]{1,0:T(8,128)}) custom-call(f32[256,256]{1,0:T(8,128)S(1)} %get-tuple-element.4.s_done, f32[512,256]{1,0:T(8,128)S(1)} %get-tuple-element.5.f_done), custom_call_target="tpu_custom_call" | custom-call | tf_op jit(solution)/shard_map/store/pallas_call | solution.py:407

commit v3 on v2

--- a/solution.py
+++ b/solution.py
@@ -8,6 +8,7 @@
 BLK = 128
 ROUNDS = 6
 ROWS = 8
+TALL = 16
 KEPT = 6
 GRANT = 32 * 1024 * 1024
 MESH = pl.DeviceIdType.MESH
@@ -55,21 +56,35 @@
     return jnp.dot(x, y, preferred_element_type=F32)
 
 
+def thirds(x):
+    high, rest = halves(x)
+    return high, rest, (x - high.astype(F32) - rest.astype(F32)).astype(jnp.bfloat16)
+
+
 def times(x_split, split):
     x_high, x_low = x_split
-    high, low = split
-    return dot(x_high, high) + (dot(x_low, high) + dot(x_high, low))
+    high, low = split[:2]
+    width = high.shape[1]
+    if width == BLK:
+        beside = jnp.concatenate([high, low], axis=1)
+        first, second = dot(x_high, beside), dot(x_low, beside)
+        small = first[:, width:] + (second[:, :width] + second[:, width:])
+        large = first[:, :width]
+    else:
+        small = dot(x_low, high) + dot(x_high, low)
+        large = dot(x_high, high)
+    if len(split) == 3:
+        small = small + dot(x_high, split[2])
+    return large + small
 
 
 def products(x, y):
-    x_high, x_low = halves(x)
-    y_high, y_low = halves(y)
-
-    def columns(a, b):
-        return lax.dot_general(a, b, (((0,), (0,)), ((), ())), preferred_element_type=F32)
-
-    small = columns(x_high, y_low) + columns(x_low, y_high)
-    return columns(x_high, y_high) + (small + columns(x_low, y_low))
+    x_parts, y_parts = thirds(x.T), thirds(y)
+    count = x.shape[1]
+    by_high = dot(jnp.concatenate(x_parts, axis=0), y_parts[0])
+    by_middle = dot(jnp.concatenate(x_parts[:2], axis=0), y_parts[1])
+    smallest = by_high[2 * count:] + by_middle[count:] + dot(x_parts[0], y_parts[2])
+    return by_high[:count] + ((by_high[count:2 * count] + by_middle[:count]) + smallest)
 
 
 def backwards(x):
@@ -157,14 +172,26 @@
     return tuple(zip(*out))
 
 
+def turn_columns(part, cos, sin):
+    to_u, to_v = part
+    return to_u * cos - to_v * sin, to_u * sin + to_v * cos
+
+
+def shift_columns(part):
+    to_u, to_v = part
+    lane = iota((TALL, BLK), 1)
+    moved_u = pltpu.roll(next_lane(to_u), 1, 0)
+    moved_v = pltpu.roll(jnp.where(lane == 1, previous_lane(to_u), previous_lane(to_v)), TALL - 1, 0)
+    return jnp.where(lane == BLK - 1, to_v, moved_u), jnp.where(lane == 0, to_v, moved_v)
+
+
 def solve(uu, uv, vu, vv):
-    tall = (2 * BLK, BLK)
-    row, lane = iota(tall, 0), iota(tall, 1)
-    q_u = jnp.where(row == lane, 1.0, 0.0).astype(F32)
-    q_v = jnp.where(row == 2 * BLK - 1 - lane, 1.0, 0.0).astype(F32)
+    one = jnp.where(iota((TALL, BLK), 0) == ROWS, 1.0, 0.0).astype(F32)
+    none = jnp.zeros((TALL, BLK), F32)
+    parts = [(one, none), (none, one)]
     for round_index in range(ROUNDS):
         cos, sin = angles(round_index, uu, uv, vv)
-        q_u, q_v = q_u * cos - q_v * sin, q_u * sin + q_v * cos
+        parts = [turn_columns(part, cos, sin) for part in parts]
         if round_index + 1 == ROUNDS:
             break
         near = [jnp.broadcast_to(x, (ROWS, BLK)) for x in (cos, sin)]
@@ -178,39 +205,63 @@
             b, d = b * cos - d * sin, b * sin + d * cos
             new.append((a, b, c, d))
         uu, uv, vu, vv = shift_pairs(*zip(*new))
-        q_u, q_v = (
-            jnp.where(lane == BLK - 1, q_v, next_lane(q_u)),
-            jnp.where(lane == 0, q_v, jnp.where(lane == 1, previous_lane(q_u), previous_lane(q_v))),
-        )
-    return q_u, q_v
-
-
-def block_columns(q_u, q_v, lower):
+        parts = [shift_columns(part) for part in parts]
+    return parts
+
+
+def column_places(lower):
     last_round = ROUNDS - 1
     lane = iota((1, BLK), 1)
-    upper_index = jnp.where(lane >= last_round, lane - last_round, last_round - lane)
-    from_u = jnp.where(lane < last_round, BLK - last_round + lane, 0)
+    upper_place = jnp.where(lane >= last_round, lane - last_round, last_round - lane)
+    from_u = BLK - last_round + lane
     from_v = jnp.where(lane == BLK - 1, 0, BLK - 1 + last_round - lane)
-    lower_index = jnp.where(lane < last_round, from_u, from_v)
-    index = jnp.where(lower, lower_index, upper_index)
+    place = jnp.where(lower, jnp.where(lane < last_round, from_u, from_v), upper_place)
     first = lane < last_round
     in_u = (first & lower) | (jnp.logical_not(first) & jnp.logical_not(lower))
-    return jnp.where(in_u, lanes(q_u, index), lanes(q_v, index))
+    return in_u, place
+
+
+def block_columns(parts, lower):
+    in_u, place = column_places(lower)
+    return [jnp.where(in_u, lanes(to_u, place), lanes(to_v, place)) for to_u, to_v in parts]
+
+
+def spread_rows(near, start):
+    tall = jnp.concatenate([near, jnp.zeros((ROWS, BLK), F32)], axis=0)
+    for bit in (1, 2, 4):
+        tall = jnp.where((start & bit) != 0, pltpu.roll(tall, bit, 0), tall)
+    tile = start >> 3
+    out = []
+    for at in range(BLK // ROWS):
+        rows = jnp.where(tile == at - 1, tall[2 * ROWS:], 0.0)
+        rows = jnp.where(tile == at, tall[ROWS:2 * ROWS], rows)
+        out.append(jnp.where(tile == at + 1, tall[:ROWS], rows))
+    return out
+
+
+def whole_columns(near, lower):
+    place = column_places(lower)[1]
+    from_u, from_v = near
+    flip = ROWS - 1 - iota((ROWS, BLK), 0)
+    from_v = [jnp.take_along_axis(x, flip, axis=0) for x in (from_v[ROWS:], from_v[:ROWS])]
+    tiles = spread_rows(from_u, place) + spread_rows(jnp.concatenate(from_v, axis=0), BLK - place)
+    return jnp.concatenate(tiles, axis=0)
 
 
 def kernel(
     rows, pairs,
     s_in, f_in, s_out, f_out,
     s_own, f_own, s_half, f_half, s_pair, f_pair, s_split, f_split, s_done, f_done, bands, place, total,
+    s_other, columns_own, columns_in,
     load_sem, store_sem, sum_send, sum_recv, move_send, move_recv,
 ):
+    load_s = pltpu.make_async_copy(s_in, s_own, load_sem.at[0])
+    load_f = pltpu.make_async_copy(f_in, f_own, load_sem.at[1])
+    with jax.named_scope("loads"):
+        load_s.start()
+        load_f.start()
     row, col = lax.axis_index("row"), lax.axis_index("col")
     last = pairs - 1
-
-    load_s = pltpu.make_async_copy(s_in, s_own, load_sem.at[0])
-    load_f = pltpu.make_async_copy(f_in, f_own, load_sem.at[1])
-    load_s.start()
-    load_f.start()
 
     up_to = jnp.where(col == 0, 1, jnp.where(col == last, last - 1, jnp.where(col == last - 1, last, col + 2)))
     up_pair = jnp.where(col >= last - 1, 1, 0)
@@ -220,7 +271,8 @@
     low_half = jnp.where(col == 0, 0, 1)
     stays_a = jnp.where(col == 0, 0, 1)
     stays_b = jnp.where(col == 0, 1, 0)
-    half_b = jnp.where(col == last, 1, 0)
+    own_half = (stays_a, jnp.where(col == last, 1, 0))
+    other_lower = ((col == 0) | (col == 2), col < last - 1)
 
     barrier = pltpu.get_barrier_semaphore()
     peers = [lax.rem(row + rows // 2 * (d % 2) + d // 2, rows) for d in range(rows - 1, 0, -1)]
@@ -263,51 +315,81 @@
     with jax.named_scope("entry"):
         pl.semaphore_wait(barrier, rows + 1)
     share(0)
+
+    def move(kind, at, source, target, pair, to):
+        return pltpu.make_async_remote_copy(
+            src_ref=source, dst_ref=target, send_sem=move_send.at[kind, at], recv_sem=move_recv.at[kind, pair],
+            device_id={"col": to}, device_id_type=MESH,
+        )
+
+    s_moves = [
+        move(0, at, s_own, s_other.at[pair], pair, to)
+        for at, (pair, to) in enumerate(((up_pair, up_to), (low_pair, low_to)))
+    ]
+    for copy in s_moves:
+        copy.start()
     blocks = summed(0)
     with jax.named_scope("solve_first"):
-        q_u, q_v = solve(*blocks)
-        split = [halves(block_columns(q_u, q_v, lower)) for lower in (False, True)]
-        split = [jnp.concatenate(parts, axis=1) for parts in zip(*split)]
-
-    def move(kind, half, at, target, pair, half_at, to):
-        return pltpu.make_async_remote_copy(
-            src_ref=half.at[at], dst_ref=target.at[pair, half_at],
-            send_sem=move_send.at[kind, at], recv_sem=move_recv.at[kind, pair],
-            device_id={"col": to}, device_id_type=MESH,
+        parts = solve(*blocks)
+        columns = [block_columns(parts, lower) for lower in (False, True)]
+        for at, near in enumerate(columns):
+            columns_own[at, :TALL], columns_own[at, TALL:] = near
+    column_moves = [
+        move(2, at, columns_own.at[at], columns_in.at[pair], pair, to)
+        for at, (pair, to) in enumerate(((up_pair, up_to), (low_pair, low_to)))
+    ]
+    for copy in column_moves:
+        copy.start()
+    with jax.named_scope("rotation_first"):
+        split = thirds(
+            jnp.concatenate([whole_columns(near, lower) for near, lower in zip(columns, (False, True))], axis=1)
         )
 
-    def moves(kind, half, target):
-        return (
-            move(kind, half, 0, target, up_pair, up_half, up_to),
-            move(kind, half, 1, target, low_pair, low_half, low_to),
-        )
-
-    def rotate(own, half, target):
-        moved = times(halves(own[...]), split)
+    def rotate(own, half, parts):
+        moved = times(halves(own[...]), parts)
         half[0] = moved[:, :BLK]
         half[1] = moved[:, BLK:]
 
     def stay(half, target):
-        target[0, stays_a] = half[stays_a]
-        target[1, half_b] = half[stays_b]
-
-    s_moves, f_moves = moves(0, s_half, s_pair), moves(1, f_half, f_pair)
+        target[0, own_half[0]] = half[stays_a]
+        target[1, own_half[1]] = half[stays_b]
+
+    f_moves = [
+        move(1, 0, f_half.at[0], f_pair.at[up_pair, up_half], up_pair, up_to),
+        move(1, 1, f_half.at[1], f_pair.at[low_pair, low_half], low_pair, low_to),
+    ]
     with jax.named_scope("apply_slab"):
-        rotate(s_own, s_half, s_pair)
-    for copy in s_moves:
-        copy.start()
+        rotate(s_own, s_half, split)
+        stay(s_half, s_pair)
     load_f.wait()
     with jax.named_scope("apply_factor"):
-        stay(s_half, s_pair)
-        rotate(f_own, f_half, f_pair)
+        rotate(f_own, f_half, split[:2])
         stay(f_half, f_pair)
 
-    def arrived(kind, half, target, pair):
-        move(kind, half, 0, target, pair, 0, up_to).wait_recv()
+    def arrived(kind, target, pair):
+        move(kind, 0, target, target, pair, up_to).wait_recv()
+
+    def keep_halves(whole, pair, split):
+        split[0, pair], split[1, pair] = halves(whole)
 
     for pair in range(2):
         with jax.named_scope("slab_arrival"):
-            arrived(0, s_half, s_pair, pair)
+            arrived(0, s_other.at[pair], pair)
+        with jax.named_scope("split_other"):
+            keep_halves(s_other[pair], pair, s_split)
+    def pick(choices, at):
+        return jnp.where(at == 0, choices[0], choices[1])
+
+    first = jnp.where((col == pairs // 2) | (col == pairs // 2 + 1), 1, 0)
+    order = (first, 1 - first)
+    for pair in order:
+        with jax.named_scope("columns_arrival"):
+            arrived(2, columns_in.at[pair], pair)
+        with jax.named_scope("rotation_other"):
+            near = [columns_in[pair, :TALL], columns_in[pair, TALL:]]
+            rotation = thirds(whole_columns(near, pick(other_lower, pair)))
+        with jax.named_scope("apply_other"):
+            s_pair[pair, 1 - pick(own_half, pair)] = times((s_split[0, pair], s_split[1, pair]), rotation)
         with jax.named_scope("gram_second"):
             form(1 + pair, s_pair[pair, 0], s_pair[pair, 1])
         share(1 + pair)
@@ -316,29 +398,31 @@
 
     lower_of = (col == 1, col != last)
 
-    def keep_halves(target, pair, split):
-        whole = jnp.concatenate([target[pair, 0], target[pair, 1]], axis=1)
-        split[0, pair], split[1, pair] = halves(whole)
+    def joined(target, pair):
+        return jnp.concatenate([target[pair, 0], target[pair, 1]], axis=1)
 
     def finish(split, done, pair, rotation):
-        done[:, pair * BLK:(pair + 1) * BLK] = times((split[0, pair], split[1, pair]), rotation)
+        at = pl.ds(pl.multiple_of(pair * BLK, BLK), BLK)
+        done[:, at] = times((split[0, pair], split[1, pair]), rotation)
 
     with jax.named_scope("split_slab"):
         for pair in range(2):
-            keep_halves(s_pair, pair, s_split)
-    for pair in range(2):
+            keep_halves(joined(s_pair, pair), pair, s_split)
+    for step, pair in enumerate(order):
         blocks = summed(1 + pair)
         with jax.named_scope("solve_second"):
-            q_u, q_v = solve(*blocks)
-            rotation = halves(block_columns(q_u, q_v, lower_of[pair]))
+            parts = solve(*blocks)
+        with jax.named_scope("rotation_second"):
+            lower = pick(lower_of, pair)
+            rotation = halves(whole_columns(block_columns(parts, lower), lower))
         with jax.named_scope("finish_slab"):
             finish(s_split, s_done, pair, rotation)
-        if pair == 0:
+        if step == 0:
             for at in range(2):
                 with jax.named_scope("factor_arrival"):
-                    arrived(1, f_half, f_pair, at)
+                    arrived(1, f_half.at[0], at)
                 with jax.named_scope("split_factor"):
-                    keep_halves(f_pair, at, f_split)
+                    keep_halves(joined(f_pair, at), at, f_split)
         with jax.named_scope("finish_factor"):
             finish(f_split, f_done, pair, rotation)
     store_s = pltpu.make_async_copy(s_done, s_out, store_sem.at[0])
@@ -347,7 +431,7 @@
     store_f.start()
 
     with jax.named_scope("last_waits"):
-        for copy in s_moves + f_moves:
+        for copy in s_moves + column_moves + f_moves:
             copy.wait_send()
         for at in range(3):
             rest = bands.at[at, pl.ds(0, rows - 1)]
@@ -394,12 +478,15 @@
                 pltpu.VMEM((3, rows, 4 * KEPT, BLK), F32),
                 pltpu.VMEM((4, 2 * ROWS, BLK), F32),
                 pltpu.VMEM((3, 4 * ROWS, BLK), F32),
+                pltpu.VMEM((2,) + matrix.shape, F32),
+                pltpu.VMEM((2, 2 * TALL, BLK), F32),
+                pltpu.VMEM((2, 2 * TALL, BLK), F32),
                 pltpu.SemaphoreType.DMA((2,)),
                 pltpu.SemaphoreType.DMA((2,)),
                 pltpu.SemaphoreType.DMA((3,)),
                 pltpu.SemaphoreType.DMA((3,)),
-                pltpu.SemaphoreType.DMA((2, 2)),
-                pltpu.SemaphoreType.DMA((2, 2)),
+                pltpu.SemaphoreType.DMA((3, 2)),
+                pltpu.SemaphoreType.DMA((3, 2)),
             ],
             compiler_params=pltpu.CompilerParams(collective_id=0, has_side_effects=True, vmem_limit_bytes=GRANT),
             name="tournament",

time: 44.3 us -> 38.7 us (0.87)
  the two profiles are of different devices: /device:TPU:12 before, /device:TPU:4 now
where the time goes in v3:
time: 38.7 us; the launch traced here: 38.6 us
  Pallas kernels  37.9 us (98%)
  between operations  0.64 us (2%)
    pallas_call x1, Pallas kernels, shards(): pl.pallas_call(lambda *refs: kernel(rows, pairs, *refs), out_shape=(pltpu...  37 us
    pallas_call x1, Pallas kernels, shards(): pl.pallas_call(store, out_shape=(pltpu.HBM(matrix.shape, F32), pltpu.HBM(...  0.9 us

profile of v3, /device:TPU:4, one launch (start us, length us, event | category | flops | bytes accessed | tf_op | source)
XLA Modules:
  0.0 38.6 jit_solution(14081116196533407313)
XLA Ops:
  0.6 37.0 %tournament.1 = (f32[256,256]{1,0:T(8,128)S(1)}, f32[512,256]{1,0:T(8,128)S(1)}) custom-call(f32[256,256]{1,0:T(8,128)} %refs_0_.1, f32[512,256]{1,0:T(8,128)} %refs_1_.1), custom_call_target="tpu_custom_call" | custom-call | tf_op jit(solution)/shard_map/tournament/pallas_call | solution.py:459
  37.7 0.9 %store.1 = (f32[256,256]{1,0:T(8,128)}, f32[512,256]{1,0:T(8,128)}) custom-call(f32[256,256]{1,0:T(8,128)S(1)} %get-tuple-element.4.s_done, f32[512,256]{1,0:T(8,128)S(1)} %get-tuple-element.5.f_done), custom_call_target="tpu_custom_call" | custom-call | tf_op jit(solution)/shard_map/store/pallas_call | solution.py:494

commit v4 on v3

--- a/solution.py
+++ b/solution.py
@@ -91,9 +91,16 @@
     return lanes(x, BLK - 1 - iota((1, BLK), 1))
 
 
-def diagonals(x, place):
-    place[...] = pltpu.roll(x, 1, 1, stride=1, stride_axis=0).T[:2 * ROWS]
-    return place[pl.ds(0, ROWS, stride=2)], place[pl.ds(1, ROWS, stride=2)]
+def diagonals(blocks, place):
+    lane = iota((BLK, BLK), 1)
+    beside = pltpu.roll(blocks[0], 1, 1, stride=1, stride_axis=0)
+    for at, block in enumerate(blocks[1:], 1):
+        turned = pltpu.roll(block, 1 + at * TALL, 1, stride=1, stride_axis=0)
+        beside = jnp.where(lane >= at * TALL, turned, beside)
+    place[...] = beside.T[:len(blocks) * TALL]
+    return [
+        tuple(place[pl.ds(at * TALL + odd, ROWS, stride=2)] for odd in range(2)) for at in range(len(blocks))
+    ]
 
 
 def flipped_rows(x):
@@ -122,7 +129,7 @@
     right = jnp.concatenate([backwards(upper), lower], axis=1)
     gram = products(left, right)
     blocks = (gram[:BLK, :BLK], gram[:BLK, BLK:], gram[BLK:, :BLK], gram[BLK:, BLK:])
-    return [pack(*diagonals(block, place.at[at])) for at, block in enumerate(blocks)]
+    return [pack(*pair) for pair in diagonals(blocks, place)]
 
 
 def angles(round_index, uu, uv, vv):
@@ -188,12 +195,12 @@
 def solve(uu, uv, vu, vv):
     one = jnp.where(iota((TALL, BLK), 0) == ROWS, 1.0, 0.0).astype(F32)
     none = jnp.zeros((TALL, BLK), F32)
-    parts = [(one, none), (none, one)]
-    for round_index in range(ROUNDS):
+    parts = ((one, none), (none, one))
+
+    def turn(round_index, state):
+        (uu, uv, vu, vv), parts = state
         cos, sin = angles(round_index, uu, uv, vv)
-        parts = [turn_columns(part, cos, sin) for part in parts]
-        if round_index + 1 == ROUNDS:
-            break
+        parts = tuple(turn_columns(part, cos, sin) for part in parts)
         near = [jnp.broadcast_to(x, (ROWS, BLK)) for x in (cos, sin)]
         new = []
         for at in range(2):
@@ -204,9 +211,11 @@
             a, c = a * cos - c * sin, a * sin + c * cos
             b, d = b * cos - d * sin, b * sin + d * cos
             new.append((a, b, c, d))
-        uu, uv, vu, vv = shift_pairs(*zip(*new))
-        parts = [shift_columns(part) for part in parts]
-    return parts
+        return shift_pairs(*zip(*new)), tuple(shift_columns(part) for part in parts)
+
+    blocks, parts = lax.fori_loop(0, ROUNDS - 1, turn, ((uu, uv, vu, vv), parts))
+    cos, sin = angles(ROUNDS - 1, blocks[0], blocks[1], blocks[3])
+    return [turn_columns(part, cos, sin) for part in parts]
 
 
 def column_places(lower):
@@ -275,7 +284,11 @@
     other_lower = ((col == 0) | (col == 2), col < last - 1)
 
     barrier = pltpu.get_barrier_semaphore()
-    peers = [lax.rem(row + rows // 2 * (d % 2) + d // 2, rows) for d in range(rows - 1, 0, -1)]
+    ring = rows // 2
+    side, place_at = row // ring, lax.rem(row, ring)
+    steps = [(across, step) for step in range(ring) for across in (1, 0) if across or step]
+    steps.sort(key=lambda s: -min(s[1], ring - s[1]))
+    peers = [lax.rem(side + across, 2) * ring + lax.rem(place_at + step, ring) for across, step in steps]
     with jax.named_scope("greet"):
         for peer in peers:
             pl.semaphore_signal(barrier, inc=1, device_id={"row": peer}, device_id_type=MESH)
@@ -380,7 +393,7 @@
     def pick(choices, at):
         return jnp.where(at == 0, choices[0], choices[1])
 
-    first = jnp.where((col == pairs // 2) | (col == pairs // 2 + 1), 1, 0)
+    first = jnp.where((col >= pairs // 2) & (col < pairs // 2 + 4), 1, 0)
     order = (first, 1 - first)
     for pair in order:
         with jax.named_scope("columns_arrival"):
@@ -408,7 +421,7 @@
     with jax.named_scope("split_slab"):
         for pair in range(2):
             keep_halves(joined(s_pair, pair), pair, s_split)
-    for step, pair in enumerate(order):
+    for pair in order:
         blocks = summed(1 + pair)
         with jax.named_scope("solve_second"):
             parts = solve(*blocks)
@@ -417,12 +430,10 @@
             rotation = halves(whole_columns(block_columns(parts, lower), lower))
         with jax.named_scope("finish_slab"):
             finish(s_split, s_done, pair, rotation)
-        if step == 0:
-            for at in range(2):
-                with jax.named_scope("factor_arrival"):
-                    arrived(1, f_half.at[0], at)
-                with jax.named_scope("split_factor"):
-                    keep_halves(joined(f_pair, at), at, f_split)
+        with jax.named_scope("factor_arrival"):
+            arrived(1, f_half.at[0], pair)
+        with jax.named_scope("split_factor"):
+            keep_halves(joined(f_pair, pair), pair, f_split)
         with jax.named_scope("finish_factor"):
             finish(f_split, f_done, pair, rotation)
     store_s = pltpu.make_async_copy(s_done, s_out, store_sem.at[0])
@@ -476,7 +487,7 @@
                 pltpu.VMEM(matrix.shape, F32),
                 pltpu.VMEM(right_factor.shape, F32),
                 pltpu.VMEM((3, rows, 4 * KEPT, BLK), F32),
-                pltpu.VMEM((4, 2 * ROWS, BLK), F32),
+                pltpu.VMEM((4 * TALL, BLK), F32),
                 pltpu.VMEM((3, 4 * ROWS, BLK), F32),
                 pltpu.VMEM((2,) + matrix.shape, F32),
                 pltpu.VMEM((2, 2 * TALL, BLK), F32),

time: 38.7 us -> 37.8 us (0.977)
  the two profiles are of different devices: /device:TPU:4 before, /device:TPU:6 now
where the time goes in v4:
time: 37.8 us; the launch traced here: 37.6 us
  Pallas kernels  37 us (98%)
  between operations  0.64 us (2%)
    pallas_call x1, Pallas kernels, shards(): pl.pallas_call(lambda *refs: kernel(rows, pairs, *refs), out_shape=(pltpu...  36.1 us
    pallas_call x1, Pallas kernels, shards(): pl.pallas_call(store, out_shape=(pltpu.HBM(matrix.shape, F32), pltpu.HBM(...  0.9 us

profile of v4, /device:TPU:6, one launch (start us, length us, event | category | flops | bytes accessed | tf_op | source)
XLA Modules:
  0.0 37.6 jit_solution(1611974381534890206)
XLA Ops:
  0.6 36.1 %tournament.1 = (f32[256,256]{1,0:T(8,128)S(1)}, f32[512,256]{1,0:T(8,128)S(1)}) custom-call(f32[256,256]{1,0:T(8,128)} %refs_0_.1, f32[512,256]{1,0:T(8,128)} %refs_1_.1), custom_call_target="tpu_custom_call" | custom-call | tf_op jit(solution)/shard_map/tournament/pallas_call | solution.py:470
  36.7 0.9 %store.1 = (f32[256,256]{1,0:T(8,128)}, f32[512,256]{1,0:T(8,128)}) custom-call(f32[256,256]{1,0:T(8,128)S(1)} %get-tuple-element.4.s_done, f32[512,256]{1,0:T(8,128)S(1)} %get-tuple-element.5.f_done), custom_call_target="tpu_custom_call" | custom-call | tf_op jit(solution)/shard_map/store/pallas_call | solution.py:505

commit v5 on v4

--- a/solution.py
+++ b/solution.py
@@ -385,17 +385,16 @@
     def keep_halves(whole, pair, split):
         split[0, pair], split[1, pair] = halves(whole)
 
-    for pair in range(2):
+    def pick(choices, at):
+        return jnp.where(at == 0, choices[0], choices[1])
+
+    first = jnp.where((col >= pairs // 2) & (col < pairs // 2 + 4), 1, 0)
+    order = (first, 1 - first)
+    for pair in order:
         with jax.named_scope("slab_arrival"):
             arrived(0, s_other.at[pair], pair)
         with jax.named_scope("split_other"):
             keep_halves(s_other[pair], pair, s_split)
-    def pick(choices, at):
-        return jnp.where(at == 0, choices[0], choices[1])
-
-    first = jnp.where((col >= pairs // 2) & (col < pairs // 2 + 4), 1, 0)
-    order = (first, 1 - first)
-    for pair in order:
         with jax.named_scope("columns_arrival"):
             arrived(2, columns_in.at[pair], pair)
         with jax.named_scope("rotation_other"):

time: 37.8 us -> 37.7 us (level)
  the two profiles are of different devices: /device:TPU:6 before, /device:TPU:4 now
where the time goes in v5:
time: 37.7 us; the launch traced here: 37.5 us
  Pallas kernels  36.9 us (98%)
  between operations  0.64 us (2%)
    pallas_call x1, Pallas kernels, shards(): pl.pallas_call(lambda *refs: kernel(rows, pairs, *refs), out_shape=(pltpu...  36 us
    pallas_call x1, Pallas kernels, shards(): pl.pallas_call(store, out_shape=(pltpu.HBM(matrix.shape, F32), pltpu.HBM(...  0.9 us

profile of v5, /device:TPU:4, one launch (start us, length us, event | category | flops | bytes accessed | tf_op | source)
XLA Modules:
  0.0 37.5 jit_solution(18256880787918736531)
XLA Ops:
  0.6 36.0 %tournament.1 = (f32[256,256]{1,0:T(8,128)S(1)}, f32[512,256]{1,0:T(8,128)S(1)}) custom-call(f32[256,256]{1,0:T(8,128)} %refs_0_.1, f32[512,256]{1,0:T(8,128)} %refs_1_.1), custom_call_target="tpu_custom_call" | custom-call | tf_op jit(solution)/shard_map/tournament/pallas_call | solution.py:469
  36.6 0.9 %store.1 = (f32[256,256]{1,0:T(8,128)}, f32[512,256]{1,0:T(8,128)}) custom-call(f32[256,256]{1,0:T(8,128)S(1)} %get-tuple-element.4.s_done, f32[512,256]{1,0:T(8,128)S(1)} %get-tuple-element.5.f_done), custom_call_target="tpu_custom_call" | custom-call | tf_op jit(solution)/shard_map/store/pallas_call | solution.py:504

commit v6 on v5

--- a/solution.py
+++ b/solution.py
@@ -97,7 +97,7 @@
     for at, block in enumerate(blocks[1:], 1):
         turned = pltpu.roll(block, 1 + at * TALL, 1, stride=1, stride_axis=0)
         beside = jnp.where(lane >= at * TALL, turned, beside)
-    place[...] = beside.T[:len(blocks) * TALL]
+    place[:len(blocks) * TALL] = beside.T[:len(blocks) * TALL]
     return [
         tuple(place[pl.ds(at * TALL + odd, ROWS, stride=2)] for odd in range(2)) for at in range(len(blocks))
     ]
@@ -307,8 +307,7 @@
             send(at, own, own, peer).start()
 
     def form(at, upper, lower):
-        for block, packed in enumerate(gram_bands(upper, lower, place)):
-            bands[at, row, KEPT * block:KEPT * (block + 1)] = packed
+        bands[at, row] = jnp.concatenate(gram_bands(upper, lower, place), axis=0)
 
     def summed(at):
         rest = bands.at[at, pl.ds(0, rows - 1)]
@@ -486,7 +485,7 @@
                 pltpu.VMEM(matrix.shape, F32),
                 pltpu.VMEM(right_factor.shape, F32),
                 pltpu.VMEM((3, rows, 4 * KEPT, BLK), F32),
-                pltpu.VMEM((4 * TALL, BLK), F32),
+                pltpu.VMEM((4 * TALL + ROWS, BLK), F32),
                 pltpu.VMEM((3, 4 * ROWS, BLK), F32),
                 pltpu.VMEM((2,) + matrix.shape, F32),
                 pltpu.VMEM((2, 2 * TALL, BLK), F32),

time: 37.7 us -> 37.6 us (level)
  no operation moved by 1% of the time
where the time goes in v6:
time: 37.6 us; the launch traced here: 37.5 us
  Pallas kernels  36.9 us (98%)
  between operations  0.64 us (2%)
    pallas_call x1, Pallas kernels, shards(): pl.pallas_call(lambda *refs: kernel(rows, pairs, *refs), out_shape=(pltpu...  36 us
    pallas_call x1, Pallas kernels, shards(): pl.pallas_call(store, out_shape=(pltpu.HBM(matrix.shape, F32), pltpu.HBM(...  0.9 us

profile of v6, /device:TPU:4, one launch (start us, length us, event | category | flops | bytes accessed | tf_op | source)
XLA Modules:
  0.0 37.5 jit_solution(14800086671122034824)
XLA Ops:
  0.6 36.0 %tournament.1 = (f32[256,256]{1,0:T(8,128)S(1)}, f32[512,256]{1,0:T(8,128)S(1)}) custom-call(f32[256,256]{1,0:T(8,128)} %refs_0_.1, f32[512,256]{1,0:T(8,128)} %refs_1_.1), custom_call_target="tpu_custom_call" | custom-call | tf_op jit(solution)/shard_map/tournament/pallas_call | solution.py:468
  36.6 0.9 %store.1 = (f32[256,256]{1,0:T(8,128)}, f32[512,256]{1,0:T(8,128)}) custom-call(f32[256,256]{1,0:T(8,128)S(1)} %get-tuple-element.4.s_done, f32[512,256]{1,0:T(8,128)S(1)} %get-tuple-element.5.f_done), custom_call_target="tpu_custom_call" | custom-call | tf_op jit(solution)/shard_map/store/pallas_call | solution.py:503

commit v7 on v6

--- a/solution.py
+++ b/solution.py
@@ -137,13 +137,12 @@
     spread = vv[0][0:1] - uu[0][0:1]
     across = 2.0 * uv[0][0:1]
     width = jnp.abs(spread)
-    scale = jnp.maximum(jnp.abs(across), width)
-    live = scale > 0
-    inverse = 1.0 / jnp.where(live, scale, 1.0)
-    across = across * inverse
-    width = jnp.where(live, width * inverse, 1.0)
-    root = lax.rsqrt(across * across + width * width)
-    square = 0.5 + 0.5 * width * root
+    scale = jnp.where(jnp.maximum(jnp.abs(across), width) < 1e-12, 1e20, 1.0)
+    across = across * scale
+    width = width * scale
+    norm = across * across + width * width
+    root = jnp.where(norm > 0, lax.rsqrt(norm), 0.0)
+    square = jnp.where(norm > 0, 0.5 + 0.5 * width * root, 1.0)
     root_cosine = lax.rsqrt(square)
     cosine = square * root_cosine
     sine = 0.5 * across * root * root_cosine
@@ -260,7 +259,7 @@
 def kernel(
     rows, pairs,
     s_in, f_in, s_out, f_out,
-    s_own, f_own, s_half, f_half, s_pair, f_pair, s_split, f_split, s_done, f_done, bands, place, total,
+    s_own, f_own, s_half, f_half, s_pair, f_pair, s_split, f_split, s_done, f_done, bands, place,
     s_other, columns_own, columns_in,
     load_sem, store_sem, sum_send, sum_recv, move_send, move_recv,
 ):
@@ -316,10 +315,9 @@
         whole = bands[at, 0]
         for d in range(1, rows):
             whole = whole + bands[at, d]
-        total[at, 0:4 * KEPT] = whole
-        return [unpack(total[at, KEPT * block:KEPT * block + ROWS]) for block in range(4)]
-
-    total[...] = jnp.zeros(total.shape, F32)
+        whole = jnp.concatenate([whole, jnp.zeros((ROWS, BLK), F32)], axis=0)
+        return [unpack(whole[KEPT * block:KEPT * block + ROWS]) for block in range(4)]
+
     with jax.named_scope("load_slab"):
         load_s.wait()
     with jax.named_scope("gram_first"):
@@ -419,21 +417,29 @@
     with jax.named_scope("split_slab"):
         for pair in range(2):
             keep_halves(joined(s_pair, pair), pair, s_split)
-    for pair in order:
+    for step, pair in enumerate(order):
         blocks = summed(1 + pair)
         with jax.named_scope("solve_second"):
             parts = solve(*blocks)
         with jax.named_scope("rotation_second"):
             lower = pick(lower_of, pair)
             rotation = halves(whole_columns(block_columns(parts, lower), lower))
-        with jax.named_scope("finish_slab"):
-            finish(s_split, s_done, pair, rotation)
+        if step == 0:
+            with jax.named_scope("finish_slab"):
+                finish(s_split, s_done, pair, rotation)
         with jax.named_scope("factor_arrival"):
             arrived(1, f_half.at[0], pair)
         with jax.named_scope("split_factor"):
             keep_halves(joined(f_pair, pair), pair, f_split)
         with jax.named_scope("finish_factor"):
-            finish(f_split, f_done, pair, rotation)
+            if step == 0:
+                finish(f_split, f_done, pair, rotation)
+            else:
+                stacked = [jnp.concatenate([s_split[i, pair], f_split[i, pair]], axis=0) for i in range(2)]
+                result = times(stacked, rotation)
+                at = pl.ds(pl.multiple_of(pair * BLK, BLK), BLK)
+                s_done[:, at] = result[:s_done.shape[0]]
+                f_done[:, at] = result[s_done.shape[0]:]
     store_s = pltpu.make_async_copy(s_done, s_out, store_sem.at[0])
     store_f = pltpu.make_async_copy(f_done, f_out, store_sem.at[1])
     store_s.start()
@@ -486,7 +492,6 @@
                 pltpu.VMEM(right_factor.shape, F32),
                 pltpu.VMEM((3, rows, 4 * KEPT, BLK), F32),
                 pltpu.VMEM((4 * TALL + ROWS, BLK), F32),
-                pltpu.VMEM((3, 4 * ROWS, BLK), F32),
                 pltpu.VMEM((2,) + matrix.shape, F32),
                 pltpu.VMEM((2, 2 * TALL, BLK), F32),
                 pltpu.VMEM((2, 2 * TALL, BLK), F32),

time: 37.6 us -> 37.4 us (level)
  no operation moved by 1% of the time
where the time goes in v7:
time: 37.4 us; the launch traced here: 37.3 us
  Pallas kernels  36.6 us (98%)
  between operations  0.64 us (2%)
    pallas_call x1, Pallas kernels, shards(): pl.pallas_call(lambda *refs: kernel(rows, pairs, *refs), out_shape=(pltpu...  35.7 us
    pallas_call x1, Pallas kernels, shards(): pl.pallas_call(store, out_shape=(pltpu.HBM(matrix.shape, F32), pltpu.HBM(...  0.9 us

profile of v7, /device:TPU:4, one launch (start us, length us, event | category | flops | bytes accessed | tf_op | source)
XLA Modules:
  0.0 37.3 jit_solution(17481179249929250589)
XLA Ops:
  0.6 35.7 %tournament.1 = (f32[256,256]{1,0:T(8,128)S(1)}, f32[512,256]{1,0:T(8,128)S(1)}) custom-call(f32[256,256]{1,0:T(8,128)} %refs_0_.1, f32[512,256]{1,0:T(8,128)} %refs_1_.1), custom_call_target="tpu_custom_call" | custom-call | tf_op jit(solution)/shard_map/tournament/pallas_call | solution.py:474
  36.4 0.9 %store.1 = (f32[256,256]{1,0:T(8,128)}, f32[512,256]{1,0:T(8,128)}) custom-call(f32[256,256]{1,0:T(8,128)S(1)} %get-tuple-element.4.s_done, f32[512,256]{1,0:T(8,128)S(1)} %get-tuple-element.5.f_done), custom_call_target="tpu_custom_call" | custom-call | tf_op jit(solution)/shard_map/store/pallas_call | solution.py:508
